TPU v7x, 32 devices: a whole 2x2x4 slice. The times are simulated.
32 devices in a mesh: dp: 4 (over z), rows: 2 (over core), tensor: 4 (over y, x).
Axes of the slice: x: 2, y: 2, z: 4, core: 2. Of those that a mesh axis runs over, the one named last changes fastest.
Arguments:
- section_input: bfloat16 [4, 36, 24576], P('dp', 'rows', 'tensor'), may hold values from -6 to 6
- conv_weights: bfloat16 [6, 512, 4608], P(None, 'tensor'), may hold values from -0.09375 to 0.09375
- norm_gains: float32 [6, 512], P(None, 'tensor'), may hold values from 0.25 to 1.75
- norm_shifts: float32 [6, 512], P(None, 'tensor'), may hold values from -0.5 to 0.5
- out_grad: bfloat16 [4, 36, 24576], P('dp', 'rows', 'tensor'), may hold values from -6 to 6
- out_mask: int32 [4, 36, 48], P('dp', 'rows'), may hold values from 0 to 1, as said below
Outputs:
- section_output: bfloat16 [4, 36, 24576], P('dp', 'rows', 'tensor')
- input_grad: float32 [4, 36, 24576], P('dp', 'rows', 'tensor')
- conv_grads: float32 [6, 512, 4608], P(None, 'tensor')
- gain_grads: float32 [6, 512], P(None, 'tensor')
- shift_grads: float32 [6, 512], P(None, 'tensor')
Inputs may be any that keep to these rules, and one draw needn't show every extreme that they name: `out_mask`: 0 or 1; the share of ones differs from image to image, one of 1, 1/2, 1/4 or 1/8 in law.
All inputs are finite; a program needn't handle non-finite values.
Results may differ from a plain program's by a relative error of at most 0.034.
Values may be sent and summed in bfloat16 or wider, within the bound.
No kernel may reach another device: no remote copies, remote signals or barrier semaphores. Data moves between devices by JAX's collectives and lax.ppermute only.
A program may use at most 128 MiB of HBM per device.

v0:
```python
import functools

import jax
import jax.numpy as jnp
from jax import lax
from jax.experimental import pallas as pl
from jax.experimental.pallas import tpu as pltpu
from jax.sharding import PartitionSpec as P

EPS = 1e-05


def padded_2(cells, sides, width):
    for axis, dim in sides:
        count = lax.axis_size(axis)
        ends = count - 1
        head = lax.slice_in_dim(cells, 0, width, axis=dim)
        tail = lax.slice_in_dim(cells, cells.shape[dim] - width, cells.shape[dim], axis=dim)
        cells = jnp.concatenate(
            [
                lax.ppermute(tail, axis, [(i, (i + 1) % count) for i in range(ends)]),
                cells,
                lax.ppermute(head, axis, [((i + 1) % count, i) for i in range(ends)]),
            ],
            axis=dim,
        )
    return cells


def to_maps(flat, width):
    count, high, merged = flat.shape
    return flat.reshape(count, high, merged // width, width).transpose(0, 1, 3, 2)


def from_maps(maps):
    count, high, wide, chans = maps.shape
    return maps.transpose(0, 1, 3, 2).reshape(count, high, chans * wide)


def spatial_conv(padded, kernel):
    return lax.conv_general_dilated(
        padded,
        kernel,
        (1, 1),
        ((0, 0), (1, 1)),
        dimension_numbers=("NHWC", "HWIO", "NHWC"),
        preferred_element_type=jnp.float32,
    )


def flipped(kernel):
    return jnp.transpose(kernel[::-1, ::-1], (0, 1, 3, 2))


def pool_unpool(values):
    count, high, wide, chans = values.shape
    blocks = values.reshape(count, high // 2, 2, wide // 2, 2, chans)
    pooled = jax.nn.logsumexp(blocks, axis=(2, 4), keepdims=True)
    return (jnp.exp(blocks - pooled) * pooled).reshape(values.shape)


def moments(conv_out, total_pixels):
    summed = lax.psum(jnp.sum(conv_out, axis=(0, 1, 2)), ("dp", "rows"))
    mean = summed / total_pixels
    spread = lax.psum(jnp.sum(jnp.square(conv_out - mean), axis=(0, 1, 2)), ("dp", "rows"))
    var = spread / total_pixels
    return (mean, lax.rsqrt(var + EPS))


def kernel_grad(whole, dconv):
    images, rows_here, width, chans = dconv.shape
    widened = jnp.pad(whole, ((0, 0), (0, 0), (1, 1), (0, 0)))
    stacked = []
    for row_off in range(3):
        line = []
        for col_off in range(3):
            window = widened[:, row_off : row_off + rows_here, col_off : col_off + width, :]
            line.append(
                jnp.einsum("bhwc,bhwo->co", window, dconv, preferred_element_type=jnp.float32)
            )
        stacked.append(jnp.stack(line))
    return jnp.stack(stacked)


def generic_local(section_input, conv_weights, norm_gains, norm_shifts, out_grad, out_mask):
    width = out_mask.shape[2]
    images, rows_here = (out_mask.shape[0], out_mask.shape[1])
    total_pixels = float(images * rows_here * width * lax.axis_size("dp") * lax.axis_size("rows"))
    layers, out_here, flat_in = conv_weights.shape
    chans_in = flat_in // 9
    kernels_hwio = conv_weights.reshape(layers, out_here, 3, 3, chans_in).transpose(0, 2, 3, 4, 1)
    middle = layers // 2
    kept = []
    acting = to_maps(section_input, width)
    current = acting.astype(jnp.float32)
    pre_pool = current
    for index in range(layers):
        if index == middle:
            pre_pool = current
            acting = pool_unpool(pre_pool).astype(jnp.bfloat16)
        padded = padded_2(acting, (("rows", 1),), 1)
        whole = lax.all_gather(padded, "tensor", axis=3, tiled=True)
        conv_out = spatial_conv(whole, kernels_hwio[index])
        mean, rstd = moments(conv_out, total_pixels)
        normed = (conv_out - mean) * rstd
        shifted = normed * norm_gains[index] + norm_shifts[index]
        current = jax.nn.silu(shifted)
        acting = current.astype(jnp.bfloat16)
        kept.append((whole, normed, shifted, rstd))
    grad = to_maps(out_grad, width).astype(jnp.float32) * out_mask[..., None].astype(jnp.float32)
    kernel_list = [None] * layers
    gain_list = [None] * layers
    shift_list = [None] * layers
    for index in range(layers - 1, -1, -1):
        whole, normed, shifted, rstd = kept[index]
        unused, pull_silu = jax.vjp(jax.nn.silu, shifted)
        dshift = pull_silu(grad)[0]
        gain_sum, shift_sum = lax.psum(
            (jnp.sum(dshift * normed, axis=(0, 1, 2)), jnp.sum(dshift, axis=(0, 1, 2))),
            ("dp", "rows"),
        )
        gain_list[index] = gain_sum
        shift_list[index] = shift_sum
        dconv = (
            norm_gains[index]
            * rstd
            * (dshift - shift_sum / total_pixels - normed * gain_sum / total_pixels)
        ).astype(jnp.bfloat16)
        summed_kernel = lax.psum(
            kernel_grad(whole, dconv).astype(jnp.bfloat16), ("dp", "rows")
        ).astype(jnp.float32)
        kernel_list[index] = summed_kernel.transpose(3, 0, 1, 2).reshape(out_here, flat_in)
        grad_rim = padded_2(dconv, (("rows", 1),), 1)
        partial_terms = spatial_conv(grad_rim, flipped(kernels_hwio[index]))
        grad_in = lax.psum_scatter(
            partial_terms.astype(jnp.bfloat16), "tensor", scatter_dimension=3, tiled=True
        ).astype(jnp.float32)
        if index == middle:
            unused, pull_pool = jax.vjp(pool_unpool, pre_pool)
            grad = pull_pool(grad_in)[0]
        else:
            grad = grad_in
    return (
        from_maps(acting),
        from_maps(grad),
        jnp.stack(kernel_list),
        jnp.stack(gain_list),
        jnp.stack(shift_list),
    )


GROUPS = 4
LANES = 128
WIDE = 48
CHANS = GROUPS * LANES
F32 = jnp.float32
BF16 = jnp.bfloat16
VMEM = pl.BlockSpec(memory_space=pltpu.VMEM)
SMEM = pl.BlockSpec(memory_space=pltpu.SMEM)
ANY = pl.BlockSpec(memory_space=pltpu.HBM)
FREE = pl.BlockSpec(memory_space=pl.ANY)
LITTLE = pl.CostEstimate(flops=1024, bytes_accessed=1024, transcendentals=0)
PARAMS = pltpu.CompilerParams(vmem_limit_bytes=20 * 1024 * 1024)


def in_hbm(value):
    return pltpu.with_memory_space_constraint(value, pltpu.HBM)


def fits_kernels(mesh):
    return mesh.shape["tensor"] == GROUPS and mesh.shape["rows"] == 2 and mesh.shape["dp"] == 4


def sigmoid(v):
    return 0.5 * jnp.tanh(0.5 * v) + 0.5


def swap_columns(v):
    column = lax.broadcasted_iota(jnp.int32, v.shape, 0)
    return jnp.where(column % 2 == 0, pltpu.roll(v, WIDE - 1, 0), pltpu.roll(v, 1, 0))


def soft_parts(h):
    top = jnp.maximum(h[0], h[1])
    top = jnp.maximum(top, swap_columns(top))
    e0, e1 = jnp.exp(h[0] - top), jnp.exp(h[1] - top)
    total = e0 + e1
    total = total + swap_columns(total)
    pooled = top + jnp.log(total)
    inverse = 1.0 / total
    return e0 * inverse, e1 * inverse, pooled


def soft(h):
    h = h.reshape(2, WIDE, LANES)
    q0, q1, pooled = soft_parts(h)
    return jnp.concatenate([q0 * pooled, q1 * pooled], axis=0)


def soft_pull(h, grad):
    h = h.reshape(2, WIDE, LANES)
    grad = grad.reshape(2, WIDE, LANES)
    q0, q1, pooled = soft_parts(h)
    mix = q0 * grad[0] + q1 * grad[1]
    mix = mix + swap_columns(mix)
    return jnp.concatenate(
        [q0 * (pooled * (grad[0] - mix) + mix), q1 * (pooled * (grad[1] - mix) + mix)], axis=0
    )


def norm_tables(st, group, i_own, i_oth, n_local, total):
    parts = st.shape[0]
    group = 0 if st.shape[1] == 1 else group
    blocks = [st[i, group] for i in range(parts)]
    summed = functools.reduce(jnp.add, blocks)
    mean = summed[0:1] / parts
    apart = functools.reduce(jnp.add, [jnp.square(b - mean) for b in blocks])
    rstd = lax.rsqrt((summed[1:2] + n_local * apart[0:1]) / total + EPS)
    return rstd, (st[i_own, group, 0:1] - mean) * rstd, (st[i_oth, group, 0:1] - mean) * rstd


def left_right(y0, y1, y2):
    rows = y0.shape[0]
    column = lax.broadcasted_iota(jnp.int32, y0.shape, 0) % WIDE
    before = jnp.where(column == 0, 0.0, pltpu.roll(y0, 1, 0))
    after = jnp.where(column == WIDE - 1, 0.0, pltpu.roll(y2, rows - 1, 0))
    return before + y1 + after


def lane_of(group):
    return pl.multiple_of(group * LANES, LANES)


def edge_start(n_own, edge, half):
    return pl.multiple_of((1 - half) * (n_own - edge), WIDE)


def pair_rows(j):
    return pl.ds(pl.multiple_of(j * 2 * WIDE, 2 * WIDE), 2 * WIDE)


def fold(v):
    return jnp.sum(v.reshape(v.shape[0] // 8, 8, LANES), axis=0)


def fwd_kernel(first, pool, layer, total, edge_out, *refs):
    pos, zall = refs[0], refs[1]
    if first:
        w_hbm = refs[2]
    else:
        st, gss, w_hbm = refs[2], refs[3:7], refs[7]
    hb_out, zc_out, edge_ref, st_out, hb, w, y, z, tab, hs, sem = refs[-11:]
    load = pltpu.make_async_copy(w_hbm.at[layer], w, sem.at[0])
    load.start()
    save = pltpu.make_async_copy(hb, hb_out.at[layer], sem.at[1])
    t, r = pos[0], pos[1]
    n_own = z.shape[0]
    halo_at = pl.multiple_of((1 - r) * (n_own + WIDE), WIDE)
    zero_at = pl.multiple_of(r * (n_own + WIDE), WIDE)
    hb[pl.ds(zero_at, WIDE), :] = jnp.zeros((WIDE, CHANS), BF16)
    edge = zall.shape[0] - n_own
    if not first:
        for k in range(GROUPS):
            group = t ^ k
            rstd, own, oth = norm_tables(st, group, pos[2], pos[3], float(n_own), total)
            gain, shift = gss[k][layer - 1 : layer, :], gss[k][layer + 7 : layer + 8, :]
            tab[group, 0:1] = rstd * gain
            tab[group, 1:2] = own * gain + shift
            tab[group, 2:3] = oth * gain + shift

    def act(values, group, which):
        if first:
            return values
        n = values.astype(F32) * tab[group, 0:1, :] + tab[group, which : which + 1, :]
        h = n * sigmoid(n)
        return soft(h) if pool else h

    def body(j, carry):
        at = pl.multiple_of(j * 2 * WIDE, 2 * WIDE)
        for group in range(GROUPS):
            lanes = slice(group * LANES, (group + 1) * LANES)
            h = act(zall[pl.ds(at, 2 * WIDE), lanes], group, 1)
            hb[pl.ds(pl.multiple_of(at + WIDE, WIDE), 2 * WIDE), lanes] = h.astype(BF16)
        return carry

    lax.fori_loop(0, n_own // (2 * WIDE), body, 0)
    for group in range(GROUPS):
        lanes = slice(group * LANES, (group + 1) * LANES)
        h = act(zall[n_own : n_own + edge, lanes], group, 2)
        if edge > WIDE:
            hs[...] = h
            h = hs[pl.ds(pl.multiple_of(r * WIDE, WIDE), WIDE), :]
        hb[pl.ds(halo_at, WIDE), lanes] = h.astype(BF16)
    save.start()
    load.wait()
    lhs = jnp.concatenate([hb[i * WIDE : i * WIDE + n_own, :] for i in range(3)], axis=1)
    rhs = jnp.concatenate(
        [
            jnp.concatenate([w[:, (3 * i + s) * CHANS : (3 * i + s + 1) * CHANS] for i in range(3)], axis=1)
            for s in range(3)
        ],
        axis=0,
    )
    y[...] = lax.dot_general(lhs, rhs, (((1,), (1,)), ((), ())), preferred_element_type=F32)

    def add_up(j, acc):
        rows = pair_rows(j)
        v = left_right(y[rows, 0:128], y[rows, 128:256], y[rows, 256:384])
        z[rows, :] = v
        return acc + fold(v)

    steps = n_own // (2 * WIDE)
    summed = lax.fori_loop(0, steps, add_up, jnp.zeros((8, LANES), F32))
    mean = jnp.sum(summed, axis=0, keepdims=True) / n_own

    def centre(j, acc):
        rows = pair_rows(j)
        v = z[rows, :] - mean
        z[rows, :] = v
        zc_out[rows, :] = v.astype(BF16)
        return acc + fold(jnp.square(v))

    apart = lax.fori_loop(0, steps, centre, jnp.zeros((8, LANES), F32))
    sums = jnp.concatenate([mean, jnp.sum(apart, axis=0, keepdims=True)], axis=0)
    for i in range(st_out.shape[0]):
        st_out[i] = sums
    edge_ref[...] = zc_out[pl.ds(edge_start(n_own, edge_out, r), edge_out), :]
    zc_out[n_own : n_own + edge_out, :] = jnp.zeros((edge_out, LANES), BF16)
    save.wait()


def fwd_step(layer, pool, edge_out, total, pos, slots, st, tables, weights, kept, n_own, devices, ties):
    first = st is None
    layers = weights.shape[0]
    extra = () if first else (st, *tables)
    return pl.pallas_call(
        functools.partial(fwd_kernel, first, pool, layer, total, edge_out),
        out_shape=(
            pltpu.HBM((layers, n_own + 2 * WIDE, CHANS), BF16),
            pltpu.VMEM((n_own + edge_out, LANES), BF16),
            pltpu.VMEM((edge_out, LANES), BF16),
            pltpu.VMEM((devices, 2, LANES), F32),
        ),
        in_specs=[SMEM] + [VMEM] * (1 + len(extra)) + [ANY] * (1 if first else 2) + [FREE] * len(ties),
        out_specs=(ANY, VMEM, VMEM, VMEM),
        input_output_aliases={} if first else {3 + len(extra): 0},
        scratch_shapes=[
            pltpu.VMEM((n_own + 2 * WIDE, CHANS), BF16),
            pltpu.VMEM((LANES, 9 * CHANS), BF16),
            pltpu.VMEM((n_own, 3 * LANES), F32),
            pltpu.VMEM((n_own, LANES), F32),
            pltpu.VMEM((GROUPS, 8, LANES), F32),
            pltpu.VMEM((2 * WIDE, LANES), F32),
            pltpu.SemaphoreType.DMA((2,)),
        ],
        compiler_params=PARAMS,
        cost_estimate=pl.CostEstimate(
            flops=2 * n_own * 9 * CHANS * LANES, bytes_accessed=4 * 1024 * 1024, transcendentals=n_own * CHANS
        ),
        name="conv_forward",
    )(pos, slots, *extra, in_hbm(weights), *(() if first else (in_hbm(kept),)), *ties)


def below_kernel(layer, pool, total, top, *refs):
    pos, zc, st, gs = refs[:4]
    if top:
        terms, h_out, dn_out, msg, tab = refs[4:]
    else:
        terms, (dn_out, msg, tab) = refs[4:8], refs[-3:]
    n_own = dn_out.shape[0]
    rstd, own, oth = norm_tables(st, pos[0], pos[2], pos[3], float(n_own), total)
    tab[0:1], tab[1:2] = rstd, own
    tab[2:3], tab[3:4] = gs[layer : layer + 1, :], gs[layer + 8 : layer + 9, :]

    def body(j, accs):
        rows = pair_rows(j)
        xhat = zc[rows, :].astype(F32) * tab[0:1, :] + tab[1:2, :]
        n = xhat * tab[2:3, :] + tab[3:4, :]
        sig = sigmoid(n)
        h = n * sig
        if top:
            g = terms[rows, :].astype(F32)
            h_out[rows, :] = h.astype(BF16)
        else:
            g = functools.reduce(jnp.add, [term[rows, :].astype(F32) for term in terms])
        if pool:
            g = soft_pull(h, g)
        dn = g * (sig * (1.0 + n - h))
        dn_out[rows, :] = dn
        return accs[0] + fold(dn), accs[1] + fold(dn * xhat)

    zero = jnp.zeros((8, LANES), F32)
    sums = lax.fori_loop(0, n_own // (2 * WIDE), body, (zero, zero))
    sums = [jnp.sum(v, axis=0, keepdims=True) for v in sums]
    msg[0:WIDE, :] = dn_out[pl.ds(edge_start(n_own, WIDE, pos[1]), WIDE), :]
    msg[WIDE : WIDE + 8, :] = jnp.concatenate(sums + [jnp.zeros((6, LANES), F32)], axis=0)


def below_step(layer, pool, total, pos, zc, st, gs, terms, ties=()):
    n_own = terms[0].shape[0]
    top = len(terms) == 1
    out_shape = [
        pltpu.VMEM((n_own, LANES), F32),
        pltpu.VMEM((WIDE + 8, LANES), F32),
    ]
    if top:
        out_shape = [jax.ShapeDtypeStruct((n_own, LANES), BF16)] + out_shape
    return pl.pallas_call(
        functools.partial(below_kernel, layer, pool, total, top),
        out_shape=tuple(out_shape),
        in_specs=[SMEM] + [VMEM] * (3 + len(terms)) + [FREE] * len(ties),
        out_specs=(VMEM,) * len(out_shape),
        scratch_shapes=[pltpu.VMEM((8, LANES), F32)],
        compiler_params=PARAMS,
        cost_estimate=LITTLE,
        name="silu_backward",
    )(pos, zc, st, gs, *terms, *ties)


def bwd_kernel(layer, total, *refs):
    pos, dn, dedge, sums, zc, st, gs, w_hbm = refs[:8]
    outs, d_out, d, w, y, tab, sem = refs[-10:-6], *refs[-6:]
    load = pltpu.make_async_copy(w_hbm.at[layer], w, sem)
    load.start()
    t, r = pos[0], pos[1]
    n_own = dn.shape[0]
    halo_at = pl.multiple_of((1 - r) * (n_own + WIDE), WIDE)
    zero_at = pl.multiple_of(r * (n_own + WIDE), WIDE)
    edge = zc.shape[0] - n_own
    d[pl.ds(zero_at, WIDE), :] = jnp.zeros((WIDE, 3 * LANES), BF16)
    rstd, own, oth = norm_tables(st, t, pos[2], pos[3], float(n_own), total)
    scale = gs[layer : layer + 1, :] * rstd
    shift_sum, gain_sum = sums[0:1, :], sums[1:2, :]
    slope = scale * gain_sum / total
    tab[0:1] = scale
    tab[1:2] = slope * rstd
    tab[2:3] = scale * shift_sum / total + slope * own
    tab[3:4] = scale * shift_sum / total + slope * oth

    def spread_columns(v, at):
        rows = v.shape[0]
        column = lax.broadcasted_iota(jnp.int32, v.shape, 0) % WIDE
        ahead = jnp.where(column == WIDE - 1, 0.0, pltpu.roll(v, rows - 1, 0))
        behind = jnp.where(column == 0, 0.0, pltpu.roll(v, 1, 0))
        d[pl.ds(at, rows), 0:128] = ahead.astype(BF16)
        d[pl.ds(at, rows), 128:256] = v.astype(BF16)
        d[pl.ds(at, rows), 256:384] = behind.astype(BF16)

    def body(j, carry):
        rows = pair_rows(j)
        v = dn[rows, :] * tab[0:1, :] - tab[2:3, :] - zc[rows, :].astype(F32) * tab[1:2, :]
        spread_columns(v, pl.multiple_of(j * 2 * WIDE + WIDE, WIDE))
        return carry

    lax.fori_loop(0, n_own // (2 * WIDE), body, 0)
    near = n_own if edge == WIDE else pl.multiple_of(n_own + r * WIDE, WIDE)
    near = zc[pl.ds(near, WIDE), :].astype(F32)
    spread_columns(dedge[0:WIDE, :] * tab[0:1, :] - tab[3:4, :] - near * tab[1:2, :], halo_at)
    d_out[...] = d[WIDE : WIDE + n_own, :]
    load.wait()
    lhs = jnp.concatenate([d[(2 - i) * WIDE : (2 - i) * WIDE + n_own, :] for i in range(3)], axis=1)
    rhs = jnp.concatenate([w[:, i * CHANS : (i + 1) * CHANS] for i in range(9)], axis=0)
    y[...] = jnp.dot(lhs, rhs, preferred_element_type=F32)

    def share(j, carry):
        rows = pair_rows(j)
        for k in range(GROUPS):
            outs[k][rows, :] = y[rows, pl.ds(lane_of(t ^ k), LANES)].astype(BF16)
        return carry

    lax.fori_loop(0, n_own // (2 * WIDE), share, 0)


def bwd_step(layer, total, pos, dn, dedge, sums, zc, st, gs, weights, ties):
    n_own = dn.shape[0]
    part = pltpu.VMEM((n_own, LANES), BF16)
    return pl.pallas_call(
        functools.partial(bwd_kernel, layer, total),
        out_shape=(
            part,
            part,
            part,
            part,
            pltpu.VMEM((n_own, 3 * LANES), BF16),
        ),
        in_specs=[SMEM] + [VMEM] * 6 + [ANY] + [FREE] * len(ties),
        out_specs=(VMEM,) * 5,
        scratch_shapes=[
            pltpu.VMEM((n_own + 2 * WIDE, 3 * LANES), BF16),
            pltpu.VMEM((LANES, 9 * CHANS), BF16),
            pltpu.VMEM((n_own, CHANS), F32),
            pltpu.VMEM((8, LANES), F32),
            pltpu.SemaphoreType.DMA,
        ],
        compiler_params=PARAMS,
        cost_estimate=LITTLE,
        name="conv_backward",
    )(pos, dn, dedge, sums, zc, st, gs, in_hbm(weights), *ties)


def last_kernel(t0, t1, t2, t3, *refs):
    out = refs[-1]

    def body(j, carry):
        rows = pair_rows(j)
        out[rows, :] = functools.reduce(jnp.add, [term[rows, :].astype(F32) for term in (t0, t1, t2, t3)])
        return carry

    lax.fori_loop(0, out.shape[0] // (2 * WIDE), body, 0)


def last_step(terms, ties):
    return pl.pallas_call(
        last_kernel,
        out_shape=jax.ShapeDtypeStruct(terms[0].shape, F32),
        in_specs=[VMEM] * 4 + [FREE] * len(ties),
        out_specs=VMEM,
        compiler_params=PARAMS,
        cost_estimate=LITTLE,
        name="add_terms",
    )(*terms, *ties)


def halves_kernel(keep, got, out):
    out[...] = (keep[...].astype(F32) + got[...].astype(F32)).astype(BF16)


def add_halves(keep, got):
    return pl.pallas_call(
        halves_kernel,
        out_shape=jax.ShapeDtypeStruct(keep.shape, BF16),
        in_specs=[VMEM] * 2,
        out_specs=VMEM,
        compiler_params=PARAMS,
        cost_estimate=LITTLE,
        name="add_halves",
    )(keep, got)


def wgrad_kernel(layer, pos, d, hb_hbm, *refs):
    keep, send, hb, grad, sem = refs[-5:]
    load = pltpu.make_async_copy(hb_hbm.at[layer], hb, sem)
    load.start()
    n_own = d.shape[0]
    lhs = d[...]
    load.wait()
    for i in range(3):
        part = lax.dot_general(
            lhs, hb[i * WIDE : i * WIDE + n_own, :], (((0,), (0,)), ((), ())), preferred_element_type=F32
        ).astype(BF16)
        for s in range(3):
            grad[:, (3 * i + s) * CHANS : (3 * i + s + 1) * CHANS] = part[s * LANES : (s + 1) * LANES]
    half = LANES // 2
    keep[...] = grad[pl.ds(pl.multiple_of(pos[1] * half, half), half), :]
    send[...] = grad[pl.ds(pl.multiple_of((1 - pos[1]) * half, half), half), :]


def wgrad_step(layer, pos, d, kept, ties):
    half = pltpu.VMEM((LANES // 2, 9 * CHANS), BF16)
    return pl.pallas_call(
        functools.partial(wgrad_kernel, layer),
        out_shape=(half, half),
        in_specs=[SMEM, VMEM, ANY] + [FREE] * len(ties),
        out_specs=(VMEM, VMEM),
        scratch_shapes=[
            pltpu.VMEM(kept.shape[1:], BF16),
            pltpu.VMEM((LANES, 9 * CHANS), BF16),
            pltpu.SemaphoreType.DMA,
        ],
        compiler_params=PARAMS,
        cost_estimate=LITTLE,
        name="kernel_gradient",
    )(pos, d, in_hbm(kept), *ties)


def place_kernel(layers, fresh, pos, *refs):
    count = 2 * len(layers)
    sources = refs[:count]
    out, held, wide, sem = refs[-4:]
    half = LANES // 2
    r = pos[1]
    loads = [pltpu.make_async_copy(sources[j], held.at[j], sem.at[j]) for j in range(count)]
    for load in loads:
        load.start()
    stores = []
    for j in range(count):
        at = pl.multiple_of((r if j % 2 == 0 else 1 - r) * half, half)
        if j >= 2:
            stores[j - 2].wait()
        loads[j].wait()
        wide[j % 2] = held[j].astype(F32)
        store = pltpu.make_async_copy(wide.at[j % 2], out.at[layers[j // 2], pl.ds(at, half)], sem.at[count + j])
        store.start()
        stores.append(store)
    for store in stores[-2:]:
        store.wait()


def place_step(layers, pos, sources, whole, count):
    half = LANES // 2
    jobs = len(sources)
    return pl.pallas_call(
        functools.partial(place_kernel, layers, whole is None),
        out_shape=pltpu.HBM((count, LANES, 9 * CHANS), F32),
        in_specs=[SMEM] + [ANY] * jobs + ([] if whole is None else [ANY]),
        out_specs=ANY,
        input_output_aliases={} if whole is None else {1 + jobs: 0},
        scratch_shapes=[
            pltpu.VMEM((jobs, half, 9 * CHANS), BF16),
            pltpu.VMEM((2, half, 9 * CHANS), F32),
            pltpu.SemaphoreType.DMA((2 * jobs,)),
        ],
        compiler_params=PARAMS,
        cost_estimate=LITTLE,
        name="place_gradients",
    )(pos, *[in_hbm(v) for v in sources], *(() if whole is None else (in_hbm(whole),)))


def swap_with(value, axis, k):
    return lax.ppermute(value, axis, [(i, i ^ k) for i in range(lax.axis_size(axis))])


def spread(own):
    return (own, *[swap_with(own, "tensor", k) for k in range(1, GROUPS)])


def halo_of_input(x, half):
    n_own = x.shape[0]
    edge = jnp.where(half == 0, x[n_own - WIDE :], x[:WIDE])
    return jnp.concatenate([x, swap_with(edge, "rows", 1)], axis=0)


def fast_local(section_input, conv_weights, norm_gains, norm_shifts, out_grad, out_mask):
    images, rows_here, width = out_mask.shape
    layers = conv_weights.shape[0]
    n_own = rows_here * width
    parts = lax.axis_size("dp") * lax.axis_size("rows")
    total = float(n_own * parts)
    t, half = lax.axis_index("tensor"), lax.axis_index("rows")
    image = lax.axis_index("dp")
    pos = jnp.stack([t, half, 2 * image + half, 2 * image + 1 - half]).astype(jnp.int32)
    middle = layers // 2
    x = to_maps(section_input, width).reshape(n_own, LANES)
    slots = lax.all_gather(halo_of_input(x, half), "tensor", axis=1, tiled=True)
    pad = jnp.zeros((8 - layers, LANES), F32)
    tables = spread(jnp.concatenate([norm_gains, pad, norm_shifts, pad], axis=0))
    top_grad = (to_maps(out_grad, width) * out_mask[..., None].astype(BF16)).reshape(n_own, LANES)

    st, kept = None, None
    halves = ("dp", "rows")
    kept_z, kept_st = [], []
    for layer in range(layers):
        last = layer + 1 == layers
        edge = 2 * WIDE if layer + 1 == middle else WIDE
        everyone = halves if last else (*halves, "tensor")
        devices = parts if last else parts * GROUPS
        kept, zc, rim, local = fwd_step(
            layer,
            layer == middle,
            edge,
            total,
            pos,
            slots,
            st,
            tables,
            conv_weights,
            kept,
            n_own,
            devices,
            (top_grad,) if layer == 2 else (),
        )
        rim = swap_with(rim, "rows", 1)
        st = lax.all_to_all(local, everyone, split_axis=0, concat_axis=0, tiled=True)
        st = st.reshape(parts, devices // parts, 2, LANES)
        zc = lax.dynamic_update_slice_in_dim(zc, rim, n_own, axis=0)
        kept_z.append(zc)
        kept_st.append(st)
        if not last:
            slots = lax.all_gather(zc, "tensor", axis=1, tiled=True)
    top = layers - 1
    h_last, dn, msg = below_step(top, False, total, pos, kept_z[top], kept_st[top], tables[0], (top_grad,))

    def with_other(values):
        return [v for mine in values for v in (mine, swap_with(mine, "rows", 1))]

    sum_list, pairs = [None] * layers, [None] * layers
    ahead, back = [[0, 1, 2, 3]], [[3, 2, 1, 0]]
    urgent = ()
    for layer in range(layers - 1, -1, -1):
        got = swap_with(msg, "rows", 1)
        sums = msg[WIDE:] + got[WIDE:]
        one, two, three = (swap_with(sums, "dp", k) for k in (1, 2, 3))
        sums = (sums + one) + (two + three)
        sum_list[layer] = sums
        *terms, d = bwd_step(
            layer, total, pos, dn, got, sums, kept_z[layer], kept_st[layer], tables[0], conv_weights, urgent
        )
        terms = (terms[0], *[swap_with(terms[k], "tensor", k) for k in range(1, GROUPS)])
        keep, send = wgrad_step(layer, pos, d, kept, ())
        other = swap_with(send, "rows", 1)
        pairs[layer] = add_halves(keep, other)
        urgent, settled = (other,), (() if layer + 1 == layers else (pairs[layer + 1],))
        if layer == 4:
            upper = lax.psum((pairs[5], pairs[4]), "dp", axis_index_groups=ahead)
        if layer == 2:
            mid = lax.psum((pairs[3], pairs[2]), "dp", axis_index_groups=back)
        if layer > 0:
            below = layer - 1
            late = (in_hbm(upper[0]),) if layer == 1 else ()
            dn, msg = below_step(
                below, layer == middle, total, pos, kept_z[below], kept_st[below], tables[0], terms, (keep, *settled, *late)
            )
        else:
            grad = last_step(terms, (pairs[0], pairs[1]))
    tied, upper = lax.optimization_barrier(((pairs[1], pairs[0]), upper))
    lower = lax.psum(tied, "dp", axis_index_groups=ahead)
    shape = (images, rows_here, width, LANES)
    grad, mid = lax.optimization_barrier((grad, mid))
    outputs = (from_maps(h_last.reshape(shape)), from_maps(grad.reshape(shape)))
    whole = place_step((5, 4, 3, 2), pos, with_other((*upper, *mid)), None, layers)
    sums = jnp.stack(sum_list)
    lower, whole, outputs, sums = lax.optimization_barrier((lower, whole, outputs, sums))
    whole = place_step((1, 0), pos, with_other(lower), whole, layers)
    return (*outputs, whole, sums[:, 1], sums[:, 0])


def solution(mesh):
    in_specs = (
        P("dp", "rows", "tensor"),
        P(None, "tensor", None),
        P(None, "tensor"),
        P(None, "tensor"),
        P("dp", "rows", "tensor"),
        P("dp", "rows", None),
    )
    out_specs = (
        P("dp", "rows", "tensor"),
        P("dp", "rows", "tensor"),
        P(None, "tensor", None),
        P(None, "tensor"),
        P(None, "tensor"),
    )
    local = fast_local if fits_kernels(mesh) else generic_local
    return jax.shard_map(local, mesh=mesh, in_specs=in_specs, out_specs=out_specs, check_vma=False)
```

profile of v0, /device:TPU:0, one launch (start us, length us, event | category | flops | bytes accessed | tf_op | source)
XLA Modules:
  0.0 426.7 jit_solution(848248074455082186)
XLA Ops:
  10.4 14.6 %all_gather.18.refs_1_ = bf16[912,512]{1,0:T(8,128)(2,1)S(1)} all-gather(bf16[912,128]{1,0:T(8,128)(2,1)S(1)} %pad_maximum_fusion), channel_id=1, replica_groups=mesh['dp'=4,'rows'=2,'tensor'=4] {'tensor'}, dimensions={1}, use_global_device_ids=true | all-gather | bytes 1167360 | tf_op jit(solution)/shard_map/all_gather | solution.py:644
  25.1 4.9 %conv_forward.6 = (bf16[6,960,512]{2,1,0:T(8,128)(2,1)}, bf16[912,128]{1,0:T(8,128)(2,1)S(1)}, bf16[48,128]{1,0:T(8,128)(2,1)S(1)}, f32[32,2,128]{2,1,0:T(2,128)}) custom-call(s32[4]{0:T(128)S(1)} %pad_add_fusion.refs_0_.pos, bf16[912,512]{1,0:T(8,128)(2,1)S(1)} %all_gather.18.refs_1_, bf16[6,128,4608]{2,1,0:T(8,128)(2,1)} %refs_7_.21), custom_call_target="tpu_custom_call" | custom-call | flops 1019215872 | bytes 4194304 | tf_op jit(solution)/shard_map/conv_forward/pallas_call | solution.py:336
  34.3 4.9 %all-to-all-start = ((f32[32,2,128]{2,1,0:T(2,128)}), f32[32,2,128]{2,1,0:T(2,128)S(1)}, u32[]{:S(2)}, u32[]{:S(2)}) async-start(f32[32,2,128]{2,1,0:T(2,128)} %get-tuple-element.99), calls=%async_computation | async-start | bytes 65536 | tf_op jit(solution)/shard_map/all_to_all | solution.py:673
  39.3 13.7 %all_gather.19.refs_1_ = bf16[912,512]{1,0:T(8,128)(2,1)S(1)} all-gather(bf16[912,128]{1,0:T(8,128)(2,1)S(1)} %constant_dynamic-update-slice_fusion.11.refs_1_.refs_4_), channel_id=1, replica_groups=mesh['dp'=4,'rows'=2,'tensor'=4] {'tensor'}, dimensions={1}, use_global_device_ids=true | all-gather | bytes 1167360 | tf_op jit(solution)/shard_map/all_gather | solution.py:679
  53.0 4.6 %conv_forward.7 = (bf16[6,960,512]{2,1,0:T(8,128)(2,1)}, bf16[912,128]{1,0:T(8,128)(2,1)S(1)}, bf16[48,128]{1,0:T(8,128)(2,1)S(1)}, f32[32,2,128]{2,1,0:T(2,128)}) custom-call(s32[4]{0:T(128)S(1)} %pad_add_fusion.refs_0_.pos, bf16[912,512]{1,0:T(8,128)(2,1)S(1)} %all_gather.19.refs_1_, ...), custom_call_target="tpu_custom_call", output_to_operand_aliasing={{0}: (8, {})} | custom-call | flops 1019215872 | bytes 4194304 | tf_op jit(solution)/shard_map/conv_forward/pallas_call | solution.py:336
  58.0 4.5 %all-to-all-start.1 = ((f32[32,2,128]{2,1,0:T(2,128)}), f32[32,2,128]{2,1,0:T(2,128)S(1)}, u32[]{:S(2)}, u32[]{:S(2)}) async-start(f32[32,2,128]{2,1,0:T(2,128)} %get-tuple-element.103), calls=%async_computation.1 | async-start | bytes 65536 | tf_op jit(solution)/shard_map/all_to_all | solution.py:673
  62.5 13.7 %all_gather.20.refs_1_ = bf16[912,512]{1,0:T(8,128)(2,1)S(1)} all-gather(bf16[912,128]{1,0:T(8,128)(2,1)S(1)} %constant_dynamic-update-slice_fusion.10.refs_1_.refs_4_), channel_id=1, replica_groups=mesh['dp'=4,'rows'=2,'tensor'=4] {'tensor'}, dimensions={1}, use_global_device_ids=true | all-gather | bytes 1167360 | tf_op jit(solution)/shard_map/all_gather | solution.py:679
  76.3 4.6 %conv_forward.8 = (bf16[6,960,512]{2,1,0:T(8,128)(2,1)}, bf16[960,128]{1,0:T(8,128)(2,1)S(1)}, bf16[96,128]{1,0:T(8,128)(2,1)S(1)}, f32[32,2,128]{2,1,0:T(2,128)}) custom-call(s32[4]{0:T(128)S(1)} %pad_add_fusion.refs_0_.pos, bf16[912,512]{1,0:T(8,128)(2,1)S(1)} %all_gather.20.refs_1_, ...), custom_call_target="tpu_custom_call", output_to_operand_aliasing={{0}: (8, {})} | custom-call | flops 1019215872 | bytes 4194304 | tf_op jit(solution)/shard_map/conv_forward/pallas_call | solution.py:336
  80.9 4.5 %all-to-all-start.2 = ((f32[32,2,128]{2,1,0:T(2,128)}), f32[32,2,128]{2,1,0:T(2,128)S(1)}, u32[]{:S(2)}, u32[]{:S(2)}) async-start(f32[32,2,128]{2,1,0:T(2,128)} %get-tuple-element.107), calls=%async_computation.2 | async-start | bytes 65536 | tf_op jit(solution)/shard_map/all_to_all | solution.py:673
  85.5 14.1 %all_gather.21.refs_1_ = bf16[960,512]{1,0:T(8,128)(2,1)S(1)} all-gather(bf16[960,128]{1,0:T(8,128)(2,1)S(1)} %constant_dynamic-update-slice_fusion.9.refs_1_.refs_4_), channel_id=1, replica_groups=mesh['dp'=4,'rows'=2,'tensor'=4] {'tensor'}, dimensions={1}, use_global_device_ids=true | all-gather | bytes 1228800 | tf_op jit(solution)/shard_map/all_gather | solution.py:679
  99.6 5.0 %conv_forward.9 = (bf16[6,960,512]{2,1,0:T(8,128)(2,1)}, bf16[912,128]{1,0:T(8,128)(2,1)S(1)}, bf16[48,128]{1,0:T(8,128)(2,1)S(1)}, f32[32,2,128]{2,1,0:T(2,128)}) custom-call(s32[4]{0:T(128)S(1)} %pad_add_fusion.refs_0_.pos, bf16[960,512]{1,0:T(8,128)(2,1)S(1)} %all_gather.21.refs_1_, ...), custom_call_target="tpu_custom_call", output_to_operand_aliasing={{0}: (8, {})} | custom-call | flops 1019215872 | bytes 4194304 | tf_op jit(solution)/shard_map/conv_forward/pallas_call | solution.py:336
  104.7 4.5 %all-to-all-start.3 = ((f32[32,2,128]{2,1,0:T(2,128)}), f32[32,2,128]{2,1,0:T(2,128)S(1)}, u32[]{:S(2)}, u32[]{:S(2)}) async-start(f32[32,2,128]{2,1,0:T(2,128)} %get-tuple-element.111), calls=%async_computation.3 | async-start | bytes 65536 | tf_op jit(solution)/shard_map/all_to_all | solution.py:673
  109.3 13.7 %all_gather.22.refs_1_ = bf16[912,512]{1,0:T(8,128)(2,1)S(1)} all-gather(bf16[912,128]{1,0:T(8,128)(2,1)S(1)} %constant_dynamic-update-slice_fusion.8.refs_1_.refs_4_), channel_id=1, replica_groups=mesh['dp'=4,'rows'=2,'tensor'=4] {'tensor'}, dimensions={1}, use_global_device_ids=true | all-gather | bytes 1167360 | tf_op jit(solution)/shard_map/all_gather | solution.py:679
  123.0 4.6 %conv_forward.10 = (bf16[6,960,512]{2,1,0:T(8,128)(2,1)}, bf16[912,128]{1,0:T(8,128)(2,1)S(1)}, bf16[48,128]{1,0:T(8,128)(2,1)S(1)}, f32[32,2,128]{2,1,0:T(2,128)}) custom-call(s32[4]{0:T(128)S(1)} %pad_add_fusion.refs_0_.pos, bf16[912,512]{1,0:T(8,128)(2,1)S(1)} %all_gather.22.refs_1_, ...), custom_call_target="tpu_custom_call", output_to_operand_aliasing={{0}: (8, {})} | custom-call | flops 1019215872 | bytes 4194304 | tf_op jit(solution)/shard_map/conv_forward/pallas_call | solution.py:336
  127.6 4.5 %all-to-all-start.4 = ((f32[32,2,128]{2,1,0:T(2,128)}), f32[32,2,128]{2,1,0:T(2,128)S(1)}, u32[]{:S(2)}, u32[]{:S(2)}) async-start(f32[32,2,128]{2,1,0:T(2,128)} %get-tuple-element.115), calls=%async_computation.4 | async-start | bytes 65536 | tf_op jit(solution)/shard_map/all_to_all | solution.py:673
  132.2 13.7 %all_gather.23.refs_1_ = bf16[912,512]{1,0:T(8,128)(2,1)S(1)} all-gather(bf16[912,128]{1,0:T(8,128)(2,1)S(1)} %constant_dynamic-update-slice_fusion.7.refs_1_.refs_4_), channel_id=1, replica_groups=mesh['dp'=4,'rows'=2,'tensor'=4] {'tensor'}, dimensions={1}, use_global_device_ids=true | all-gather | bytes 1167360 | tf_op jit(solution)/shard_map/all_gather | solution.py:679
  145.9 4.5 %conv_forward.11 = (bf16[6,960,512]{2,1,0:T(8,128)(2,1)}, bf16[912,128]{1,0:T(8,128)(2,1)S(1)}, bf16[48,128]{1,0:T(8,128)(2,1)S(1)}, f32[8,2,128]{2,1,0:T(2,128)}) custom-call(s32[4]{0:T(128)S(1)} %pad_add_fusion.refs_0_.pos, bf16[912,512]{1,0:T(8,128)(2,1)S(1)} %all_gather.23.refs_1_, ...), custom_call_target="tpu_custom_call", output_to_operand_aliasing={{0}: (8, {})} | custom-call | flops 1019215872 | bytes 4194304 | tf_op jit(solution)/shard_map/conv_forward/pallas_call | solution.py:336
  150.5 4.5 %all-to-all-start.5 = ((f32[8,2,128]{2,1,0:T(2,128)}), f32[8,2,128]{2,1,0:T(2,128)S(1)}, u32[]{:S(2)}, u32[]{:S(2)}) async-start(f32[8,2,128]{2,1,0:T(2,128)} %get-tuple-element.119), calls=%async_computation.5 | async-start | bytes 16384 | tf_op jit(solution)/shard_map/all_to_all | solution.py:673
  155.0 5.6 %all-to-all-done.5 = f32[8,2,128]{2,1,0:T(2,128)S(1)} async-done(((f32[8,2,128]{2,1,0:T(2,128)}), f32[8,2,128]{2,1,0:T(2,128)S(1)}, u32[]{:S(2)}, u32[]{:S(2)}) %all-to-all-start.5) | async-done | bytes 8224 | tf_op jit(solution)/shard_map/all_to_all | solution.py:673
  279.6 14.0 %all-reduce.9.cloned.1.call-done = (bf16[64,4608]{1,0:T(8,128)(2,1)}, bf16[64,4608]{1,0:T(8,128)(2,1)}) async-done(((bf16[64,4608]{1,0:T(8,128)(2,1)}, bf16[64,4608]{1,0:T(8,128)(2,1)}), (bf16[64,4608]{1,0:T(8,128)(2,1)}, bf16[64,4608]{1,0:T(8,128)(2,1)})) %all-reduce.9.cloned.1.call-update) | async-done | bytes 1179664 | tf_op jit(solution)/shard_map/psum | solution.py:704
  318.2 5.5 %collective-permute-done.58.t2 = bf16[864,128]{1,0:T(8,128)(2,1)S(1)} collective-permute-done((bf16[864,128]{1,0:T(8,128)(2,1)S(1)}, bf16[864,128]{1,0:T(8,128)(2,1)S(1)}, u32[]{:S(2)}, u32[]{:S(2)}) %collective-permute-start.58) | collective-permute-done | bytes 221216 | tf_op jit(solution)/shard_map/ppermute | solution.py:620
  327.2 26.5 %all-reduce.11.cloned.1.call-done = (bf16[64,4608]{1,0:T(8,128)(2,1)}, bf16[64,4608]{1,0:T(8,128)(2,1)}) async-done(((bf16[64,4608]{1,0:T(8,128)(2,1)}, bf16[64,4608]{1,0:T(8,128)(2,1)}), (bf16[64,4608]{1,0:T(8,128)(2,1)}, bf16[64,4608]{1,0:T(8,128)(2,1)})) %all-reduce.11.cloned.1.call-update) | async-done | bytes 1179664 | tf_op jit(solution)/shard_map/psum | solution.py:706
  357.4 6.5 %place_gradients.2.refs_4_ = f32[6,128,4608]{2,1,0:T(8,128)} custom-call(s32[4]{0:T(128)S(1)} %pad_add_fusion.refs_0_.pos, bf16[64,4608]{1,0:T(8,128)(2,1)} %get-tuple-element.173.refs_10_.refs_0_, bf16[64,4608]{1,0:T(8,128)(2,1)} %copy-done.2, bf16[64,4608]{1,0:T(8,128)(2,1)} %get-tuple-element.174.refs_2_, ...), custom_call_target="tpu_custom_call" | custom-call | flops 1024 | bytes 1024 | tf_op jit(solution)/shard_map/place_gradients/pallas_call | solution.py:602
  363.9 48.1 %all-reduce.7.cloned.1.call-done = (bf16[64,4608]{1,0:T(8,128)(2,1)}, bf16[64,4608]{1,0:T(8,128)(2,1)}) async-done(((bf16[64,4608]{1,0:T(8,128)(2,1)}, bf16[64,4608]{1,0:T(8,128)(2,1)}), (bf16[64,4608]{1,0:T(8,128)(2,1)}, bf16[64,4608]{1,0:T(8,128)(2,1)})) %all-reduce.7.cloned.1.call-update) | async-done | bytes 1179664 | tf_op jit(solution)/shard_map/psum | solution.py:716
  (223 shorter events, 166.8 us)
Async XLA Ops:
  30.1 22.9 %collective-permute-start.4 = (f32[16,128]{1,0:T(8,128)S(1)}, f32[16,128]{1,0:T(8,128)S(1)}, u32[]{:S(2)}, u32[]{:S(2)}) collective-permute-start(f32[16,128]{1,0:T(8,128)S(1)} %pad_maximum_fusion.1.refs_3_.refs_6_), channel_id=1, source_target_pairs={{0,3},{1,2},{2,1},{3,0},{4,7},{5,6},{6,5},{7,4},{8,11},{9,10},{10,... | collective-permute-start | bytes 24584 | tf_op jit(solution)/shard_map/ppermute | solution.py:620
  31.7 21.4 %collective-permute-start.3 = (f32[16,128]{1,0:T(8,128)S(1)}, f32[16,128]{1,0:T(8,128)S(1)}, u32[]{:S(2)}, u32[]{:S(2)}) collective-permute-start(f32[16,128]{1,0:T(8,128)S(1)} %pad_maximum_fusion.1.refs_3_.refs_6_), channel_id=1, source_target_pairs={{0,2},{1,3},{2,0},{3,1},{4,6},{5,7},{6,4},{7,5},{8,10},{9,11},{10,... | collective-permute-start | bytes 24584 | tf_op jit(solution)/shard_map/ppermute | solution.py:620
  33.1 19.9 %collective-permute-start.2 = (f32[16,128]{1,0:T(8,128)S(1)}, f32[16,128]{1,0:T(8,128)S(1)}, u32[]{:S(2)}, u32[]{:S(2)}) collective-permute-start(f32[16,128]{1,0:T(8,128)S(1)} %pad_maximum_fusion.1.refs_3_.refs_6_), channel_id=1, source_target_pairs={{0,1},{1,0},{2,3},{3,2},{4,5},{5,4},{6,7},{7,6},{8,9},{9,8},{10,11... | collective-permute-start | bytes 24584 | tf_op jit(solution)/shard_map/ppermute | solution.py:620
  34.3 18.7 %all-to-all-start = ((f32[32,2,128]{2,1,0:T(2,128)}), f32[32,2,128]{2,1,0:T(2,128)S(1)}, u32[]{:S(2)}, u32[]{:S(2)}) async-start(f32[32,2,128]{2,1,0:T(2,128)} %get-tuple-element.99), calls=%async_computation | async-start | bytes 65536 | tf_op jit(solution)/shard_map/all_to_all | solution.py:673
  58.0 18.3 %all-to-all-start.1 = ((f32[32,2,128]{2,1,0:T(2,128)}), f32[32,2,128]{2,1,0:T(2,128)S(1)}, u32[]{:S(2)}, u32[]{:S(2)}) async-start(f32[32,2,128]{2,1,0:T(2,128)} %get-tuple-element.103), calls=%async_computation.1 | async-start | bytes 65536 | tf_op jit(solution)/shard_map/all_to_all | solution.py:673
  80.9 18.7 %all-to-all-start.2 = ((f32[32,2,128]{2,1,0:T(2,128)}), f32[32,2,128]{2,1,0:T(2,128)S(1)}, u32[]{:S(2)}, u32[]{:S(2)}) async-start(f32[32,2,128]{2,1,0:T(2,128)} %get-tuple-element.107), calls=%async_computation.2 | async-start | bytes 65536 | tf_op jit(solution)/shard_map/all_to_all | solution.py:673
  104.7 18.3 %all-to-all-start.3 = ((f32[32,2,128]{2,1,0:T(2,128)}), f32[32,2,128]{2,1,0:T(2,128)S(1)}, u32[]{:S(2)}, u32[]{:S(2)}) async-start(f32[32,2,128]{2,1,0:T(2,128)} %get-tuple-element.111), calls=%async_computation.3 | async-start | bytes 65536 | tf_op jit(solution)/shard_map/all_to_all | solution.py:673
  127.6 18.3 %all-to-all-start.4 = ((f32[32,2,128]{2,1,0:T(2,128)}), f32[32,2,128]{2,1,0:T(2,128)S(1)}, u32[]{:S(2)}, u32[]{:S(2)}) async-start(f32[32,2,128]{2,1,0:T(2,128)} %get-tuple-element.115), calls=%async_computation.4 | async-start | bytes 65536 | tf_op jit(solution)/shard_map/all_to_all | solution.py:673
  179.0 14.5 %collective-permute-start.21 = (bf16[64,4608]{1,0:T(8,128)(2,1)S(1)}, bf16[64,4608]{1,0:T(8,128)(2,1)S(1)}, u32[]{:S(2)}, u32[]{:S(2)}) collective-permute-start(bf16[64,4608]{1,0:T(8,128)(2,1)S(1)} %get-tuple-element.131), channel_id=1, source_target_pairs={{0,4},{4,0},{1,5},{5,1},{2,6},{6,2},{3,7},{7,3},{8,12},{12,8},{9,1... | collective-permute-start | bytes 1769480 | tf_op jit(solution)/shard_map/ppermute | solution.py:620
  203.7 13.3 %collective-permute-start.29 = (bf16[64,4608]{1,0:T(8,128)(2,1)S(1)}, bf16[64,4608]{1,0:T(8,128)(2,1)S(1)}, u32[]{:S(2)}, u32[]{:S(2)}) collective-permute-start(bf16[64,4608]{1,0:T(8,128)(2,1)S(1)} %get-tuple-element.140), channel_id=1, source_target_pairs={{0,4},{4,0},{1,5},{5,1},{2,6},{6,2},{3,7},{7,3},{8,12},{12,8},{9,1... | collective-permute-start | bytes 1769480 | tf_op jit(solution)/shard_map/ppermute | solution.py:620
  222.8 11.0 %collective-permute-start.31 = (bf16[864,128]{1,0:T(8,128)(2,1)}, bf16[864,128]{1,0:T(8,128)(2,1)S(1)}, u32[]{:S(2)}, u32[]{:S(2)}) collective-permute-start(bf16[864,128]{1,0:T(8,128)(2,1)} %get-tuple-element.143), channel_id=1, source_target_pairs={{0,2},{1,3},{2,0},{3,1},{4,6},{5,7},{6,4},{7,5},{8,10},{9,11},{10,... | collective-permute-start | bytes 663560 | tf_op jit(solution)/shard_map/ppermute | solution.py:620
  228.9 14.4 %collective-permute-start.37 = (bf16[64,4608]{1,0:T(8,128)(2,1)}, bf16[64,4608]{1,0:T(8,128)(2,1)S(1)}, u32[]{:S(2)}, u32[]{:S(2)}) collective-permute-start(bf16[64,4608]{1,0:T(8,128)(2,1)} %get-tuple-element.149), channel_id=1, source_target_pairs={{0,4},{4,0},{1,5},{5,1},{2,6},{6,2},{3,7},{7,3},{8,12},{12,8},{9,1... | collective-permute-start | bytes 1769480 | tf_op jit(solution)/shard_map/ppermute | solution.py:620
  235.2 58.3 %all-reduce.9.cloned.1.call-start = ((), (), s32[]{:S(2)}) async-start(), calls=%async_computation.7 | async-start | bytes 2359296 | tf_op jit(solution)/shard_map/psum | solution.py:704
  247.3 10.9 %collective-permute-start.39 = (bf16[864,128]{1,0:T(8,128)(2,1)S(1)}, bf16[864,128]{1,0:T(8,128)(2,1)S(1)}, u32[]{:S(2)}, u32[]{:S(2)}) collective-permute-start(bf16[864,128]{1,0:T(8,128)(2,1)S(1)} %get-tuple-element.152), channel_id=1, source_target_pairs={{0,2},{1,3},{2,0},{3,1},{4,6},{5,7},{6,4},{7,5},{8,10},{9,11},{10,... | collective-permute-start | bytes 663560 | tf_op jit(solution)/shard_map/ppermute | solution.py:620
  253.5 13.3 %collective-permute-start.45 = (bf16[64,4608]{1,0:T(8,128)(2,1)S(1)}, bf16[64,4608]{1,0:T(8,128)(2,1)S(1)}, u32[]{:S(2)}, u32[]{:S(2)}) collective-permute-start(bf16[64,4608]{1,0:T(8,128)(2,1)S(1)} %get-tuple-element.158), channel_id=1, source_target_pairs={{0,4},{4,0},{1,5},{5,1},{2,6},{6,2},{3,7},{7,3},{8,12},{12,8},{9,1... | collective-permute-start | bytes 1769480 | tf_op jit(solution)/shard_map/ppermute | solution.py:620
  270.9 22.6 %collective-permute-start.47 = (bf16[864,128]{1,0:T(8,128)(2,1)}, bf16[864,128]{1,0:T(8,128)(2,1)S(1)}, u32[]{:S(2)}, u32[]{:S(2)}) collective-permute-start(bf16[864,128]{1,0:T(8,128)(2,1)} %get-tuple-element.163), channel_id=1, source_target_pairs={{0,1},{1,0},{2,3},{3,2},{4,5},{5,4},{6,7},{7,6},{8,9},{9,8},{10,11... | collective-permute-start | bytes 663560 | tf_op jit(solution)/shard_map/ppermute | solution.py:620
  272.5 21.1 %collective-permute-start.48 = (bf16[864,128]{1,0:T(8,128)(2,1)S(1)}, bf16[864,128]{1,0:T(8,128)(2,1)S(1)}, u32[]{:S(2)}, u32[]{:S(2)}) collective-permute-start(bf16[864,128]{1,0:T(8,128)(2,1)S(1)} %get-tuple-element.164), channel_id=1, source_target_pairs={{0,2},{1,3},{2,0},{3,1},{4,6},{5,7},{6,4},{7,5},{8,10},{9,11},{10,... | collective-permute-start | bytes 663560 | tf_op jit(solution)/shard_map/ppermute | solution.py:620
  273.0 20.5 %collective-permute-start.49 = (bf16[864,128]{1,0:T(8,128)(2,1)S(1)}, bf16[864,128]{1,0:T(8,128)(2,1)S(1)}, u32[]{:S(2)}, u32[]{:S(2)}) collective-permute-start(bf16[864,128]{1,0:T(8,128)(2,1)S(1)} %get-tuple-element.165), channel_id=1, source_target_pairs={{0,3},{1,2},{2,1},{3,0},{4,7},{5,6},{6,5},{7,4},{8,11},{9,10},{10,... | collective-permute-start | bytes 663560 | tf_op jit(solution)/shard_map/ppermute | solution.py:620
  278.5 24.6 %collective-permute-start.46 = (bf16[64,4608]{1,0:T(8,128)(2,1)}, bf16[64,4608]{1,0:T(8,128)(2,1)S(1)}, u32[]{:S(2)}, u32[]{:S(2)}) collective-permute-start(bf16[64,4608]{1,0:T(8,128)(2,1)} %get-tuple-element.161), channel_id=1, source_target_pairs={{0,4},{4,0},{1,5},{5,1},{2,6},{6,2},{3,7},{7,3},{8,12},{12,8},{9,1... | collective-permute-start | bytes 1769480 | tf_op jit(solution)/shard_map/ppermute | solution.py:620
  294.6 59.1 %all-reduce.11.cloned.1.call-start = ((), (), s32[]{:S(2)}) async-start(), calls=%async_computation.8 | async-start | bytes 2359296 | tf_op jit(solution)/shard_map/psum | solution.py:706
  311.4 12.2 %collective-permute-start.58 = (bf16[864,128]{1,0:T(8,128)(2,1)S(1)}, bf16[864,128]{1,0:T(8,128)(2,1)S(1)}, u32[]{:S(2)}, u32[]{:S(2)}) collective-permute-start(bf16[864,128]{1,0:T(8,128)(2,1)S(1)} %get-tuple-element.177), channel_id=1, source_target_pairs={{0,2},{1,3},{2,0},{3,1},{4,6},{5,7},{6,4},{7,5},{8,10},{9,11},{10,... | collective-permute-start | bytes 663560 | tf_op jit(solution)/shard_map/ppermute | solution.py:620
  323.8 88.2 %all-reduce.7.cloned.1.call-start = ((), (), s32[]{:S(2)}) async-start(), calls=%async_computation.6 | async-start | bytes 2359296 | tf_op jit(solution)/shard_map/psum | solution.py:716
  326.7 29.9 %collective-permute-start.55 = (bf16[64,4608]{1,0:T(8,128)(2,1)}, bf16[64,4608]{1,0:T(8,128)(2,1)S(1)}, u32[]{:S(2)}, u32[]{:S(2)}) collective-permute-start(bf16[64,4608]{1,0:T(8,128)(2,1)} %get-tuple-element.173.refs_10_.refs_0_), channel_id=1, source_target_pairs={{0,4},{4,0},{1,5},{5,1},{2,6},{6,2},{3,7},{7,3},{8,12},{12,8},{9,1... | collective-permute-start | bytes 1769480 | tf_op jit(solution)/shard_map/ppermute | solution.py:620
  326.7 29.9 %collective-permute-start.56 = (bf16[64,4608]{1,0:T(8,128)(2,1)}, bf16[64,4608]{1,0:T(8,128)(2,1)}, u32[]{:S(2)}, u32[]{:S(2)}) collective-permute-start(bf16[64,4608]{1,0:T(8,128)(2,1)} %get-tuple-element.174.refs_2_), channel_id=1, source_target_pairs={{0,4},{4,0},{1,5},{5,1},{2,6},{6,2},{3,7},{7,3},{8,12},{12,8},{9,1... | collective-permute-start | bytes 1769480 | tf_op jit(solution)/shard_map/ppermute | solution.py:620
  (58 other events, 400.7 us)
Sparse Core Ops, SparseCore 0:
  238.5 55.0 all-reduce.8
  297.9 55.8 all-reduce.10
  356.2 55.7 all-reduce.6
where the time goes:
time: 428 us; the launch traced here: 427 us
  waiting for transfers between devices  142 us (33%)
  Pallas kernels  94.3 us (22%)
  blocking collectives  83.7 us (20%)
  starting transfers between devices  82.6 us (19%)
  between operations  14.5 us (3%)
  local copies, waits for them, and re-layouts  9.15 us (2%)
    all_gather x5, blocking collectives, fast_local(): slots = lax.all_gather(zc, 'tensor', axis=1, tiled=True)  69.1 us
    ppermute x64, starting transfers between devices, swap_with(): lax.ppermute(value, axis, [(i, i ^ k) for i in range(lax.axis_size(axis))])  54.6 us
    psum x1, waiting for transfers between devices, fast_local(): lower = lax.psum(tied, 'dp', axis_index_groups=ahead)  48.1 us
    ppermute x64, waiting for transfers between devices, swap_with(): lax.ppermute(value, axis, [(i, i ^ k) for i in range(lax.axis_size(axis))])  46.5 us
    pallas_call x6, Pallas kernels, fwd_step(): pl.pallas_call(functools.partial(fwd_kernel, first, pool, layer, total, e...  28.1 us
    all_to_all x6, starting transfers between devices, fast_local(): lax.all_to_all(local, everyone, split_axis=0, concat_axis=0, tiled=True)  27.4 us
    psum x1, waiting for transfers between devices, fast_local(): mid = lax.psum((pairs[3], pairs[2]), 'dp', axis_index_groups=back)  26.5 us
    pallas_call x6, Pallas kernels, bwd_step(): pl.pallas_call(functools.partial(bwd_kernel, layer, total), out_shape=(pa...  21.9 us
  transfers between devices with their start and end apart: 73, of which 35 were waited for; matrix products, arithmetic and copies ran while one was open for 1% of the time, Pallas kernels for 12%

commit v1 on v0

--- a/solution.py
+++ b/solution.py
@@ -283,7 +283,7 @@
             hb[pl.ds(pl.multiple_of(at + WIDE, WIDE), 2 * WIDE), lanes] = h.astype(BF16)
         return carry
 
-    lax.fori_loop(0, n_own // (2 * WIDE), body, 0)
+    lax.fori_loop(0, n_own // (2 * WIDE), body, 0, unroll=3)
     for group in range(GROUPS):
         lanes = slice(group * LANES, (group + 1) * LANES)
         h = act(zall[n_own : n_own + edge, lanes], group, 2)
@@ -293,7 +293,6 @@
         hb[pl.ds(halo_at, WIDE), lanes] = h.astype(BF16)
     save.start()
     load.wait()
-    lhs = jnp.concatenate([hb[i * WIDE : i * WIDE + n_own, :] for i in range(3)], axis=1)
     rhs = jnp.concatenate(
         [
             jnp.concatenate([w[:, (3 * i + s) * CHANS : (3 * i + s + 1) * CHANS] for i in range(3)], axis=1)
@@ -301,7 +300,11 @@
         ],
         axis=0,
     )
-    y[...] = lax.dot_general(lhs, rhs, (((1,), (1,)), ((), ())), preferred_element_type=F32)
+    block = n_own // 3
+    for j in range(3):
+        at = j * block
+        lhs = jnp.concatenate([hb[at + i * WIDE : at + i * WIDE + block, :] for i in range(3)], axis=1)
+        y[at : at + block, :] = lax.dot_general(lhs, rhs, (((1,), (1,)), ((), ())), preferred_element_type=F32)
 
     def add_up(j, acc):
         rows = pair_rows(j)
@@ -310,7 +313,7 @@
         return acc + fold(v)
 
     steps = n_own // (2 * WIDE)
-    summed = lax.fori_loop(0, steps, add_up, jnp.zeros((8, LANES), F32))
+    summed = lax.fori_loop(0, steps, add_up, jnp.zeros((8, LANES), F32), unroll=3)
     mean = jnp.sum(summed, axis=0, keepdims=True) / n_own
 
     def centre(j, acc):
@@ -320,7 +323,7 @@
         zc_out[rows, :] = v.astype(BF16)
         return acc + fold(jnp.square(v))
 
-    apart = lax.fori_loop(0, steps, centre, jnp.zeros((8, LANES), F32))
+    apart = lax.fori_loop(0, steps, centre, jnp.zeros((8, LANES), F32), unroll=3)
     sums = jnp.concatenate([mean, jnp.sum(apart, axis=0, keepdims=True)], axis=0)
     for i in range(st_out.shape[0]):
         st_out[i] = sums
@@ -390,7 +393,7 @@
         return accs[0] + fold(dn), accs[1] + fold(dn * xhat)
 
     zero = jnp.zeros((8, LANES), F32)
-    sums = lax.fori_loop(0, n_own // (2 * WIDE), body, (zero, zero))
+    sums = lax.fori_loop(0, n_own // (2 * WIDE), body, (zero, zero), unroll=3)
     sums = [jnp.sum(v, axis=0, keepdims=True) for v in sums]
     msg[0:WIDE, :] = dn_out[pl.ds(edge_start(n_own, WIDE, pos[1]), WIDE), :]
     msg[WIDE : WIDE + 8, :] = jnp.concatenate(sums + [jnp.zeros((6, LANES), F32)], axis=0)
@@ -452,15 +455,18 @@
         spread_columns(v, pl.multiple_of(j * 2 * WIDE + WIDE, WIDE))
         return carry
 
-    lax.fori_loop(0, n_own // (2 * WIDE), body, 0)
+    lax.fori_loop(0, n_own // (2 * WIDE), body, 0, unroll=3)
     near = n_own if edge == WIDE else pl.multiple_of(n_own + r * WIDE, WIDE)
     near = zc[pl.ds(near, WIDE), :].astype(F32)
     spread_columns(dedge[0:WIDE, :] * tab[0:1, :] - tab[3:4, :] - near * tab[1:2, :], halo_at)
     d_out[...] = d[WIDE : WIDE + n_own, :]
     load.wait()
-    lhs = jnp.concatenate([d[(2 - i) * WIDE : (2 - i) * WIDE + n_own, :] for i in range(3)], axis=1)
     rhs = jnp.concatenate([w[:, i * CHANS : (i + 1) * CHANS] for i in range(9)], axis=0)
-    y[...] = jnp.dot(lhs, rhs, preferred_element_type=F32)
+    block = n_own // 2
+    for j in range(2):
+        at = j * block
+        lhs = jnp.concatenate([d[at + (2 - i) * WIDE : at + (2 - i) * WIDE + block, :] for i in range(3)], axis=1)
+        y[at : at + block, :] = jnp.dot(lhs, rhs, preferred_element_type=F32)
 
     def share(j, carry):
         rows = pair_rows(j)
@@ -468,7 +474,7 @@
             outs[k][rows, :] = y[rows, pl.ds(lane_of(t ^ k), LANES)].astype(BF16)
         return carry
 
-    lax.fori_loop(0, n_own // (2 * WIDE), share, 0)
+    lax.fori_loop(0, n_own // (2 * WIDE), share, 0, unroll=3)
 
 
 def bwd_step(layer, total, pos, dn, dedge, sums, zc, st, gs, weights, ties):
@@ -684,7 +690,7 @@
         return [v for mine in values for v in (mine, swap_with(mine, "rows", 1))]
 
     sum_list, pairs = [None] * layers, [None] * layers
-    ahead, back = [[0, 1, 2, 3]], [[3, 2, 1, 0]]
+    ahead, back = [[0, 1, 3, 2]], [[2, 3, 1, 0]]
     urgent = ()
     for layer in range(layers - 1, -1, -1):
         got = swap_with(msg, "rows", 1)
@@ -719,9 +725,10 @@
     outputs = (from_maps(h_last.reshape(shape)), from_maps(grad.reshape(shape)))
     whole = place_step((5, 4, 3, 2), pos, with_other((*upper, *mid)), None, layers)
     sums = jnp.stack(sum_list)
+    sums = (sums[:, 1], sums[:, 0])
     lower, whole, outputs, sums = lax.optimization_barrier((lower, whole, outputs, sums))
     whole = place_step((1, 0), pos, with_other(lower), whole, layers)
-    return (*outputs, whole, sums[:, 1], sums[:, 0])
+    return (*outputs, whole, *sums)
 
 
 def solution(mesh):

time: 428 us -> 426 us (level)
  transfers between devices with their start and end apart: 73 -> 73, of which waited for: 35 -> 35; matrix products, arithmetic and copies ran while one was open for 1% -> 2% of each run, Pallas kernels for 12% -> 12%
where the time goes in v1:
time: 426 us; the launch traced here: 425 us
  waiting for transfers between devices  139 us (33%)
  Pallas kernels  92.9 us (22%)
  blocking collectives  83.9 us (20%)
  starting transfers between devices  82.6 us (19%)
  between operations  14.5 us (3%)
  local copies, waits for them, and re-layouts  11.9 us (3%)
    all_gather x5, blocking collectives, fast_local(): slots = lax.all_gather(zc, 'tensor', axis=1, tiled=True)  69.3 us
    ppermute x64, starting transfers between devices, swap_with(): lax.ppermute(value, axis, [(i, i ^ k) for i in range(lax.axis_size(axis))])  54.5 us
    psum x1, waiting for transfers between devices, fast_local(): lower = lax.psum(tied, 'dp', axis_index_groups=ahead)  47.5 us
    ppermute x64, waiting for transfers between devices, swap_with(): lax.ppermute(value, axis, [(i, i ^ k) for i in range(lax.axis_size(axis))])  46.9 us
    all_to_all x6, starting transfers between devices, fast_local(): lax.all_to_all(local, everyone, split_axis=0, concat_axis=0, tiled=True)  27.4 us
    pallas_call x6, Pallas kernels, fwd_step(): pl.pallas_call(functools.partial(fwd_kernel, first, pool, layer, total, e...  26.6 us
    psum x1, waiting for transfers between devices, fast_local(): mid = lax.psum((pairs[3], pairs[2]), 'dp', axis_index_groups=back)  22.3 us
    pallas_call x6, Pallas kernels, wgrad_step(): pl.pallas_call(functools.partial(wgrad_kernel, layer), out_shape=(half, h...  21.9 us
  transfers between devices with their start and end apart: 73, of which 35 were waited for; matrix products, arithmetic and copies ran while one was open for 2% of the time, Pallas kernels for 12%

profile of v1, /device:TPU:0, one launch (start us, length us, event | category | flops | bytes accessed | tf_op | source)
XLA Modules:
  0.0 424.6 jit_solution(13186475632657031412)
XLA Ops:
  10.4 14.6 %all_gather.18.refs_1_ = bf16[912,512]{1,0:T(8,128)(2,1)S(1)} all-gather(bf16[912,128]{1,0:T(8,128)(2,1)S(1)} %pad_maximum_fusion), channel_id=1, replica_groups=mesh['dp'=4,'rows'=2,'tensor'=4] {'tensor'}, dimensions={1}, use_global_device_ids=true | all-gather | bytes 1167360 | tf_op jit(solution)/shard_map/all_gather | solution.py:650
  25.1 4.7 %conv_forward.6 = (bf16[6,960,512]{2,1,0:T(8,128)(2,1)}, bf16[912,128]{1,0:T(8,128)(2,1)S(1)}, bf16[48,128]{1,0:T(8,128)(2,1)S(1)}, f32[32,2,128]{2,1,0:T(2,128)}) custom-call(s32[4]{0:T(128)S(1)} %pad_add_fusion.refs_0_.pos, bf16[912,512]{1,0:T(8,128)(2,1)S(1)} %all_gather.18.refs_1_, bf16[6,128,4608]{2,1,0:T(8,128)(2,1)} %refs_7_.21), custom_call_target="tpu_custom_call" | custom-call | flops 1019215872 | bytes 4194304 | tf_op jit(solution)/shard_map/conv_forward/pallas_call | solution.py:339
  34.1 4.9 %all-to-all-start = ((f32[32,2,128]{2,1,0:T(2,128)}), f32[32,2,128]{2,1,0:T(2,128)S(1)}, u32[]{:S(2)}, u32[]{:S(2)}) async-start(f32[32,2,128]{2,1,0:T(2,128)} %get-tuple-element.100), calls=%async_computation | async-start | bytes 65536 | tf_op jit(solution)/shard_map/all_to_all | solution.py:679
  39.0 13.7 %all_gather.19.refs_1_ = bf16[912,512]{1,0:T(8,128)(2,1)S(1)} all-gather(bf16[912,128]{1,0:T(8,128)(2,1)S(1)} %constant_dynamic-update-slice_fusion.11.refs_1_.refs_4_), channel_id=1, replica_groups=mesh['dp'=4,'rows'=2,'tensor'=4] {'tensor'}, dimensions={1}, use_global_device_ids=true | all-gather | bytes 1167360 | tf_op jit(solution)/shard_map/all_gather | solution.py:685
  52.8 4.3 %conv_forward.7 = (bf16[6,960,512]{2,1,0:T(8,128)(2,1)}, bf16[912,128]{1,0:T(8,128)(2,1)S(1)}, bf16[48,128]{1,0:T(8,128)(2,1)S(1)}, f32[32,2,128]{2,1,0:T(2,128)}) custom-call(s32[4]{0:T(128)S(1)} %pad_add_fusion.refs_0_.pos, bf16[912,512]{1,0:T(8,128)(2,1)S(1)} %all_gather.19.refs_1_, ...), custom_call_target="tpu_custom_call", output_to_operand_aliasing={{0}: (8, {})} | custom-call | flops 1019215872 | bytes 4194304 | tf_op jit(solution)/shard_map/conv_forward/pallas_call | solution.py:339
  57.5 4.5 %all-to-all-start.1 = ((f32[32,2,128]{2,1,0:T(2,128)}), f32[32,2,128]{2,1,0:T(2,128)S(1)}, u32[]{:S(2)}, u32[]{:S(2)}) async-start(f32[32,2,128]{2,1,0:T(2,128)} %get-tuple-element.104), calls=%async_computation.1 | async-start | bytes 65536 | tf_op jit(solution)/shard_map/all_to_all | solution.py:679
  62.1 13.7 %all_gather.20.refs_1_ = bf16[912,512]{1,0:T(8,128)(2,1)S(1)} all-gather(bf16[912,128]{1,0:T(8,128)(2,1)S(1)} %constant_dynamic-update-slice_fusion.10.refs_1_.refs_4_), channel_id=1, replica_groups=mesh['dp'=4,'rows'=2,'tensor'=4] {'tensor'}, dimensions={1}, use_global_device_ids=true | all-gather | bytes 1167360 | tf_op jit(solution)/shard_map/all_gather | solution.py:685
  75.8 4.3 %conv_forward.8 = (bf16[6,960,512]{2,1,0:T(8,128)(2,1)}, bf16[960,128]{1,0:T(8,128)(2,1)S(1)}, bf16[96,128]{1,0:T(8,128)(2,1)S(1)}, f32[32,2,128]{2,1,0:T(2,128)}) custom-call(s32[4]{0:T(128)S(1)} %pad_add_fusion.refs_0_.pos, bf16[912,512]{1,0:T(8,128)(2,1)S(1)} %all_gather.20.refs_1_, ...), custom_call_target="tpu_custom_call", output_to_operand_aliasing={{0}: (8, {})} | custom-call | flops 1019215872 | bytes 4194304 | tf_op jit(solution)/shard_map/conv_forward/pallas_call | solution.py:339
  80.2 4.5 %all-to-all-start.2 = ((f32[32,2,128]{2,1,0:T(2,128)}), f32[32,2,128]{2,1,0:T(2,128)S(1)}, u32[]{:S(2)}, u32[]{:S(2)}) async-start(f32[32,2,128]{2,1,0:T(2,128)} %get-tuple-element.108), calls=%async_computation.2 | async-start | bytes 65536 | tf_op jit(solution)/shard_map/all_to_all | solution.py:679
  84.7 14.1 %all_gather.21.refs_1_ = bf16[960,512]{1,0:T(8,128)(2,1)S(1)} all-gather(bf16[960,128]{1,0:T(8,128)(2,1)S(1)} %constant_dynamic-update-slice_fusion.9.refs_1_.refs_4_), channel_id=1, replica_groups=mesh['dp'=4,'rows'=2,'tensor'=4] {'tensor'}, dimensions={1}, use_global_device_ids=true | all-gather | bytes 1228800 | tf_op jit(solution)/shard_map/all_gather | solution.py:685
  98.9 4.7 %conv_forward.9 = (bf16[6,960,512]{2,1,0:T(8,128)(2,1)}, bf16[912,128]{1,0:T(8,128)(2,1)S(1)}, bf16[48,128]{1,0:T(8,128)(2,1)S(1)}, f32[32,2,128]{2,1,0:T(2,128)}) custom-call(s32[4]{0:T(128)S(1)} %pad_add_fusion.refs_0_.pos, bf16[960,512]{1,0:T(8,128)(2,1)S(1)} %all_gather.21.refs_1_, ...), custom_call_target="tpu_custom_call", output_to_operand_aliasing={{0}: (8, {})} | custom-call | flops 1019215872 | bytes 4194304 | tf_op jit(solution)/shard_map/conv_forward/pallas_call | solution.py:339
  103.7 4.5 %all-to-all-start.3 = ((f32[32,2,128]{2,1,0:T(2,128)}), f32[32,2,128]{2,1,0:T(2,128)S(1)}, u32[]{:S(2)}, u32[]{:S(2)}) async-start(f32[32,2,128]{2,1,0:T(2,128)} %get-tuple-element.112), calls=%async_computation.3 | async-start | bytes 65536 | tf_op jit(solution)/shard_map/all_to_all | solution.py:679
  108.2 13.7 %all_gather.22.refs_1_ = bf16[912,512]{1,0:T(8,128)(2,1)S(1)} all-gather(bf16[912,128]{1,0:T(8,128)(2,1)S(1)} %constant_dynamic-update-slice_fusion.8.refs_1_.refs_4_), channel_id=1, replica_groups=mesh['dp'=4,'rows'=2,'tensor'=4] {'tensor'}, dimensions={1}, use_global_device_ids=true | all-gather | bytes 1167360 | tf_op jit(solution)/shard_map/all_gather | solution.py:685
  122.0 4.3 %conv_forward.10 = (bf16[6,960,512]{2,1,0:T(8,128)(2,1)}, bf16[912,128]{1,0:T(8,128)(2,1)S(1)}, bf16[48,128]{1,0:T(8,128)(2,1)S(1)}, f32[32,2,128]{2,1,0:T(2,128)}) custom-call(s32[4]{0:T(128)S(1)} %pad_add_fusion.refs_0_.pos, bf16[912,512]{1,0:T(8,128)(2,1)S(1)} %all_gather.22.refs_1_, ...), custom_call_target="tpu_custom_call", output_to_operand_aliasing={{0}: (8, {})} | custom-call | flops 1019215872 | bytes 4194304 | tf_op jit(solution)/shard_map/conv_forward/pallas_call | solution.py:339
  126.4 4.5 %all-to-all-start.4 = ((f32[32,2,128]{2,1,0:T(2,128)}), f32[32,2,128]{2,1,0:T(2,128)S(1)}, u32[]{:S(2)}, u32[]{:S(2)}) async-start(f32[32,2,128]{2,1,0:T(2,128)} %get-tuple-element.116), calls=%async_computation.4 | async-start | bytes 65536 | tf_op jit(solution)/shard_map/all_to_all | solution.py:679
  130.9 14.0 %all_gather.23.refs_1_ = bf16[912,512]{1,0:T(8,128)(2,1)S(1)} all-gather(bf16[912,128]{1,0:T(8,128)(2,1)S(1)} %constant_dynamic-update-slice_fusion.7.refs_1_.refs_4_), channel_id=1, replica_groups=mesh['dp'=4,'rows'=2,'tensor'=4] {'tensor'}, dimensions={1}, use_global_device_ids=true | all-gather | bytes 1167360 | tf_op jit(solution)/shard_map/all_gather | solution.py:685
  144.9 4.3 %conv_forward.11 = (bf16[6,960,512]{2,1,0:T(8,128)(2,1)}, bf16[912,128]{1,0:T(8,128)(2,1)S(1)}, bf16[48,128]{1,0:T(8,128)(2,1)S(1)}, f32[8,2,128]{2,1,0:T(2,128)}) custom-call(s32[4]{0:T(128)S(1)} %pad_add_fusion.refs_0_.pos, bf16[912,512]{1,0:T(8,128)(2,1)S(1)} %all_gather.23.refs_1_, ...), custom_call_target="tpu_custom_call", output_to_operand_aliasing={{0}: (8, {})} | custom-call | flops 1019215872 | bytes 4194304 | tf_op jit(solution)/shard_map/conv_forward/pallas_call | solution.py:339
  149.3 4.5 %all-to-all-start.5 = ((f32[8,2,128]{2,1,0:T(2,128)}), f32[8,2,128]{2,1,0:T(2,128)S(1)}, u32[]{:S(2)}, u32[]{:S(2)}) async-start(f32[8,2,128]{2,1,0:T(2,128)} %get-tuple-element.120), calls=%async_computation.5 | async-start | bytes 16384 | tf_op jit(solution)/shard_map/all_to_all | solution.py:679
  153.7 5.6 %all-to-all-done.5 = f32[8,2,128]{2,1,0:T(2,128)S(1)} async-done(((f32[8,2,128]{2,1,0:T(2,128)}), f32[8,2,128]{2,1,0:T(2,128)S(1)}, u32[]{:S(2)}, u32[]{:S(2)}) %all-to-all-start.5) | async-done | bytes 8224 | tf_op jit(solution)/shard_map/all_to_all | solution.py:679
  276.8 14.8 %all-reduce.9.cloned.1.call-done = (bf16[64,4608]{1,0:T(8,128)(2,1)}, bf16[64,4608]{1,0:T(8,128)(2,1)}) async-done(((bf16[64,4608]{1,0:T(8,128)(2,1)}, bf16[64,4608]{1,0:T(8,128)(2,1)}), (bf16[64,4608]{1,0:T(8,128)(2,1)}, bf16[64,4608]{1,0:T(8,128)(2,1)})) %all-reduce.9.cloned.1.call-update) | async-done | bytes 1179664 | tf_op jit(solution)/shard_map/psum | solution.py:710
  322.4 5.5 %collective-permute-done.58.t2 = bf16[864,128]{1,0:T(8,128)(2,1)S(1)} collective-permute-done((bf16[864,128]{1,0:T(8,128)(2,1)}, bf16[864,128]{1,0:T(8,128)(2,1)S(1)}, u32[]{:S(2)}, u32[]{:S(2)}) %collective-permute-start.58) | collective-permute-done | bytes 221216 | tf_op jit(solution)/shard_map/ppermute | solution.py:626
  329.4 22.3 %all-reduce.11.cloned.1.call-done = (bf16[64,4608]{1,0:T(8,128)(2,1)}, bf16[64,4608]{1,0:T(8,128)(2,1)}) async-done(((bf16[64,4608]{1,0:T(8,128)(2,1)}, bf16[64,4608]{1,0:T(8,128)(2,1)}), (bf16[64,4608]{1,0:T(8,128)(2,1)}, bf16[64,4608]{1,0:T(8,128)(2,1)})) %all-reduce.11.cloned.1.call-update) | async-done | bytes 1179664 | tf_op jit(solution)/shard_map/psum | solution.py:712
  356.0 6.5 %place_gradients.2.refs_4_ = f32[6,128,4608]{2,1,0:T(8,128)} custom-call(s32[4]{0:T(128)S(1)} %pad_add_fusion.refs_0_.pos, bf16[64,4608]{1,0:T(8,128)(2,1)} %get-tuple-element.174.refs_10_.refs_0_, bf16[64,4608]{1,0:T(8,128)(2,1)} %copy-done.3, bf16[64,4608]{1,0:T(8,128)(2,1)} %get-tuple-element.175.refs_2_, ...), custom_call_target="tpu_custom_call" | custom-call | flops 1024 | bytes 1024 | tf_op jit(solution)/shard_map/place_gradients/pallas_call | solution.py:608
  362.5 47.5 %all-reduce.7.cloned.1.call-done = (bf16[64,4608]{1,0:T(8,128)(2,1)}, bf16[64,4608]{1,0:T(8,128)(2,1)}) async-done(((bf16[64,4608]{1,0:T(8,128)(2,1)}, bf16[64,4608]{1,0:T(8,128)(2,1)}), (bf16[64,4608]{1,0:T(8,128)(2,1)}, bf16[64,4608]{1,0:T(8,128)(2,1)})) %all-reduce.7.cloned.1.call-update) | async-done | bytes 1179664 | tf_op jit(solution)/shard_map/psum | solution.py:722
  (225 shorter events, 169.9 us)
Async XLA Ops:
  29.9 22.9 %collective-permute-start.4 = (f32[16,128]{1,0:T(8,128)S(1)}, f32[16,128]{1,0:T(8,128)S(1)}, u32[]{:S(2)}, u32[]{:S(2)}) collective-permute-start(f32[16,128]{1,0:T(8,128)S(1)} %pad_maximum_fusion.1.refs_3_.refs_6_), channel_id=1, source_target_pairs={{0,3},{1,2},{2,1},{3,0},{4,7},{5,6},{6,5},{7,4},{8,11},{9,10},{10,... | collective-permute-start | bytes 24584 | tf_op jit(solution)/shard_map/ppermute | solution.py:626
  31.4 21.4 %collective-permute-start.3 = (f32[16,128]{1,0:T(8,128)S(1)}, f32[16,128]{1,0:T(8,128)S(1)}, u32[]{:S(2)}, u32[]{:S(2)}) collective-permute-start(f32[16,128]{1,0:T(8,128)S(1)} %pad_maximum_fusion.1.refs_3_.refs_6_), channel_id=1, source_target_pairs={{0,2},{1,3},{2,0},{3,1},{4,6},{5,7},{6,4},{7,5},{8,10},{9,11},{10,... | collective-permute-start | bytes 24584 | tf_op jit(solution)/shard_map/ppermute | solution.py:626
  32.9 19.9 %collective-permute-start.2 = (f32[16,128]{1,0:T(8,128)S(1)}, f32[16,128]{1,0:T(8,128)S(1)}, u32[]{:S(2)}, u32[]{:S(2)}) collective-permute-start(f32[16,128]{1,0:T(8,128)S(1)} %pad_maximum_fusion.1.refs_3_.refs_6_), channel_id=1, source_target_pairs={{0,1},{1,0},{2,3},{3,2},{4,5},{5,4},{6,7},{7,6},{8,9},{9,8},{10,11... | collective-permute-start | bytes 24584 | tf_op jit(solution)/shard_map/ppermute | solution.py:626
  34.1 18.7 %all-to-all-start = ((f32[32,2,128]{2,1,0:T(2,128)}), f32[32,2,128]{2,1,0:T(2,128)S(1)}, u32[]{:S(2)}, u32[]{:S(2)}) async-start(f32[32,2,128]{2,1,0:T(2,128)} %get-tuple-element.100), calls=%async_computation | async-start | bytes 65536 | tf_op jit(solution)/shard_map/all_to_all | solution.py:679
  57.5 18.3 %all-to-all-start.1 = ((f32[32,2,128]{2,1,0:T(2,128)}), f32[32,2,128]{2,1,0:T(2,128)S(1)}, u32[]{:S(2)}, u32[]{:S(2)}) async-start(f32[32,2,128]{2,1,0:T(2,128)} %get-tuple-element.104), calls=%async_computation.1 | async-start | bytes 65536 | tf_op jit(solution)/shard_map/all_to_all | solution.py:679
  80.2 18.7 %all-to-all-start.2 = ((f32[32,2,128]{2,1,0:T(2,128)}), f32[32,2,128]{2,1,0:T(2,128)S(1)}, u32[]{:S(2)}, u32[]{:S(2)}) async-start(f32[32,2,128]{2,1,0:T(2,128)} %get-tuple-element.108), calls=%async_computation.2 | async-start | bytes 65536 | tf_op jit(solution)/shard_map/all_to_all | solution.py:679
  103.7 18.3 %all-to-all-start.3 = ((f32[32,2,128]{2,1,0:T(2,128)}), f32[32,2,128]{2,1,0:T(2,128)S(1)}, u32[]{:S(2)}, u32[]{:S(2)}) async-start(f32[32,2,128]{2,1,0:T(2,128)} %get-tuple-element.112), calls=%async_computation.3 | async-start | bytes 65536 | tf_op jit(solution)/shard_map/all_to_all | solution.py:679
  126.4 18.5 %all-to-all-start.4 = ((f32[32,2,128]{2,1,0:T(2,128)}), f32[32,2,128]{2,1,0:T(2,128)S(1)}, u32[]{:S(2)}, u32[]{:S(2)}) async-start(f32[32,2,128]{2,1,0:T(2,128)} %get-tuple-element.116), calls=%async_computation.4 | async-start | bytes 65536 | tf_op jit(solution)/shard_map/all_to_all | solution.py:679
  177.7 14.4 %collective-permute-start.21 = (bf16[64,4608]{1,0:T(8,128)(2,1)S(1)}, bf16[64,4608]{1,0:T(8,128)(2,1)S(1)}, u32[]{:S(2)}, u32[]{:S(2)}) collective-permute-start(bf16[64,4608]{1,0:T(8,128)(2,1)S(1)} %get-tuple-element.132), channel_id=1, source_target_pairs={{0,4},{4,0},{1,5},{5,1},{2,6},{6,2},{3,7},{7,3},{8,12},{12,8},{9,1... | collective-permute-start | bytes 1769480 | tf_op jit(solution)/shard_map/ppermute | solution.py:626
  202.2 13.2 %collective-permute-start.29 = (bf16[64,4608]{1,0:T(8,128)(2,1)S(1)}, bf16[64,4608]{1,0:T(8,128)(2,1)S(1)}, u32[]{:S(2)}, u32[]{:S(2)}) collective-permute-start(bf16[64,4608]{1,0:T(8,128)(2,1)S(1)} %get-tuple-element.141), channel_id=1, source_target_pairs={{0,4},{4,0},{1,5},{5,1},{2,6},{6,2},{3,7},{7,3},{8,12},{12,8},{9,1... | collective-permute-start | bytes 1769480 | tf_op jit(solution)/shard_map/ppermute | solution.py:626
  227.2 14.1 %collective-permute-start.37 = (bf16[64,4608]{1,0:T(8,128)(2,1)}, bf16[64,4608]{1,0:T(8,128)(2,1)S(1)}, u32[]{:S(2)}, u32[]{:S(2)}) collective-permute-start(bf16[64,4608]{1,0:T(8,128)(2,1)} %get-tuple-element.150), channel_id=1, source_target_pairs={{0,4},{4,0},{1,5},{5,1},{2,6},{6,2},{3,7},{7,3},{8,12},{12,8},{9,1... | collective-permute-start | bytes 1769480 | tf_op jit(solution)/shard_map/ppermute | solution.py:626
  233.2 58.3 %all-reduce.9.cloned.1.call-start = ((), (), s32[]{:S(2)}) async-start(), calls=%async_computation.7 | async-start | bytes 2359296 | tf_op jit(solution)/shard_map/psum | solution.py:710
  245.3 10.8 %collective-permute-start.39 = (bf16[864,128]{1,0:T(8,128)(2,1)S(1)}, bf16[864,128]{1,0:T(8,128)(2,1)S(1)}, u32[]{:S(2)}, u32[]{:S(2)}) collective-permute-start(bf16[864,128]{1,0:T(8,128)(2,1)S(1)} %get-tuple-element.153), channel_id=1, source_target_pairs={{0,2},{1,3},{2,0},{3,1},{4,6},{5,7},{6,4},{7,5},{8,10},{9,11},{10,... | collective-permute-start | bytes 663560 | tf_op jit(solution)/shard_map/ppermute | solution.py:626
  251.5 13.2 %collective-permute-start.45 = (bf16[64,4608]{1,0:T(8,128)(2,1)S(1)}, bf16[64,4608]{1,0:T(8,128)(2,1)S(1)}, u32[]{:S(2)}, u32[]{:S(2)}) collective-permute-start(bf16[64,4608]{1,0:T(8,128)(2,1)S(1)} %get-tuple-element.159), channel_id=1, source_target_pairs={{0,4},{4,0},{1,5},{5,1},{2,6},{6,2},{3,7},{7,3},{8,12},{12,8},{9,1... | collective-permute-start | bytes 1769480 | tf_op jit(solution)/shard_map/ppermute | solution.py:626
  268.1 23.5 %collective-permute-start.47 = (bf16[864,128]{1,0:T(8,128)(2,1)S(1)}, bf16[864,128]{1,0:T(8,128)(2,1)S(1)}, u32[]{:S(2)}, u32[]{:S(2)}) collective-permute-start(bf16[864,128]{1,0:T(8,128)(2,1)S(1)} %get-tuple-element.164), channel_id=1, source_target_pairs={{0,1},{1,0},{2,3},{3,2},{4,5},{5,4},{6,7},{7,6},{8,9},{9,8},{10,11... | collective-permute-start | bytes 663560 | tf_op jit(solution)/shard_map/ppermute | solution.py:626
  269.7 21.9 %collective-permute-start.48 = (bf16[864,128]{1,0:T(8,128)(2,1)S(1)}, bf16[864,128]{1,0:T(8,128)(2,1)S(1)}, u32[]{:S(2)}, u32[]{:S(2)}) collective-permute-start(bf16[864,128]{1,0:T(8,128)(2,1)S(1)} %get-tuple-element.165), channel_id=1, source_target_pairs={{0,2},{1,3},{2,0},{3,1},{4,6},{5,7},{6,4},{7,5},{8,10},{9,11},{10,... | collective-permute-start | bytes 663560 | tf_op jit(solution)/shard_map/ppermute | solution.py:626
  270.2 21.4 %collective-permute-start.49 = (bf16[864,128]{1,0:T(8,128)(2,1)S(1)}, bf16[864,128]{1,0:T(8,128)(2,1)S(1)}, u32[]{:S(2)}, u32[]{:S(2)}) collective-permute-start(bf16[864,128]{1,0:T(8,128)(2,1)S(1)} %get-tuple-element.166), channel_id=1, source_target_pairs={{0,3},{1,2},{2,1},{3,0},{4,7},{5,6},{6,5},{7,4},{8,11},{9,10},{10,... | collective-permute-start | bytes 663560 | tf_op jit(solution)/shard_map/ppermute | solution.py:626
  275.7 25.4 %collective-permute-start.46 = (bf16[64,4608]{1,0:T(8,128)(2,1)}, bf16[64,4608]{1,0:T(8,128)(2,1)S(1)}, u32[]{:S(2)}, u32[]{:S(2)}) collective-permute-start(bf16[64,4608]{1,0:T(8,128)(2,1)} %get-tuple-element.162), channel_id=1, source_target_pairs={{0,4},{4,0},{1,5},{5,1},{2,6},{6,2},{3,7},{7,3},{8,12},{12,8},{9,1... | collective-permute-start | bytes 1769480 | tf_op jit(solution)/shard_map/ppermute | solution.py:626
  292.6 59.1 %all-reduce.11.cloned.1.call-start = ((), (), s32[]{:S(2)}) async-start(), calls=%async_computation.8 | async-start | bytes 2359296 | tf_op jit(solution)/shard_map/psum | solution.py:712
  315.4 12.5 %collective-permute-start.58 = (bf16[864,128]{1,0:T(8,128)(2,1)}, bf16[864,128]{1,0:T(8,128)(2,1)S(1)}, u32[]{:S(2)}, u32[]{:S(2)}) collective-permute-start(bf16[864,128]{1,0:T(8,128)(2,1)} %get-tuple-element.178), channel_id=1, source_target_pairs={{0,2},{1,3},{2,0},{3,1},{4,6},{5,7},{6,4},{7,5},{8,10},{9,11},{10,... | collective-permute-start | bytes 663560 | tf_op jit(solution)/shard_map/ppermute | solution.py:626
  316.9 11.0 %collective-permute-start.59 = (bf16[864,128]{1,0:T(8,128)(2,1)}, bf16[864,128]{1,0:T(8,128)(2,1)S(1)}, u32[]{:S(2)}, u32[]{:S(2)}) collective-permute-start(bf16[864,128]{1,0:T(8,128)(2,1)} %copy-done.2), channel_id=1, source_target_pairs={{0,3},{1,2},{2,1},{3,0},{4,7},{5,6},{6,5},{7,4},{8,11},{9,10},{10,... | collective-permute-start | bytes 663560 | tf_op jit(solution)/shard_map/ppermute | solution.py:626
  328.1 81.9 %all-reduce.7.cloned.1.call-start = ((), (), s32[]{:S(2)}) async-start(), calls=%async_computation.6 | async-start | bytes 2359296 | tf_op jit(solution)/shard_map/psum | solution.py:722
  328.8 26.3 %collective-permute-start.55 = (bf16[64,4608]{1,0:T(8,128)(2,1)}, bf16[64,4608]{1,0:T(8,128)(2,1)S(1)}, u32[]{:S(2)}, u32[]{:S(2)}) collective-permute-start(bf16[64,4608]{1,0:T(8,128)(2,1)} %get-tuple-element.174.refs_10_.refs_0_), channel_id=1, source_target_pairs={{0,4},{4,0},{1,5},{5,1},{2,6},{6,2},{3,7},{7,3},{8,12},{12,8},{9,1... | collective-permute-start | bytes 1769480 | tf_op jit(solution)/shard_map/ppermute | solution.py:626
  328.9 26.2 %collective-permute-start.56 = (bf16[64,4608]{1,0:T(8,128)(2,1)}, bf16[64,4608]{1,0:T(8,128)(2,1)}, u32[]{:S(2)}, u32[]{:S(2)}) collective-permute-start(bf16[64,4608]{1,0:T(8,128)(2,1)} %get-tuple-element.175.refs_2_), channel_id=1, source_target_pairs={{0,4},{4,0},{1,5},{5,1},{2,6},{6,2},{3,7},{7,3},{8,12},{12,8},{9,1... | collective-permute-start | bytes 1769480 | tf_op jit(solution)/shard_map/ppermute | solution.py:626
  (59 other events, 393.1 us)
Sparse Core Ops, SparseCore 0:
  236.5 55.0 all-reduce.8
  295.8 55.7 all-reduce.10
  354.1 55.7 all-reduce.6
